TPU v7x, 512 devices: a whole 4x4x16 slice. The times are simulated.
512 devices in a mesh: layer: 2 (over core), latent: 32 (over z_hi, y, x), token: 8 (over z_lo).
Axes of the slice: x: 4, y: 4, z: 16 (z_hi: 2, z_lo: 8; z = z_hi * 8 + z_lo), core: 2. Of those that a mesh axis runs over, the one named last changes fastest.
Arguments:
- taps: bfloat16 [2, 1792, 3584], P('layer', 'token'), may hold values from -6 to 6
- token_ids: int32 [1792], P('token'), may hold values from 2 to 255999, as said below
- enc_weight: bfloat16 [2, 3584, 8192], P('layer', 'token', 'latent'), may hold values from -0.0625 to 0.0625
- enc_bias: float32 [8192], P('latent'), may hold values from -3 to 3
- dec_weight: bfloat16 [2, 3584, 8192], P('layer', 'token', 'latent'), as said below
- dec_bias: float32 [2, 3584], P('layer'), may hold values from -3 to 3
Outputs:
- enc_grad: bfloat16 [2, 3584, 8192], P('layer', 'token', 'latent')
- dec_grad: bfloat16 [2, 3584, 8192], P('layer', 'token', 'latent')
Inputs may be any that keep to these rules, and one draw needn't show every extreme that they name: `token_ids`: id 2 marks the beginning of a document and stands at position 0; all other ids are 3 or more. `dec_weight`: entries of order 8192^-0.5.
All inputs are finite; a program needn't handle non-finite values.
Results may differ from a plain program's by a relative error of at most 0.014.
Values may be sent and summed in bfloat16 or wider, within the bound.
A program may use at most 64 MiB of HBM per device.

v0:
```python
import math
import jax
import jax.numpy as jnp
from jax import lax
from jax.sharding import PartitionSpec as P

KNEE_WIDTH = 0.5
SPARSITY = 0.5
BEGIN_TOKEN = 2


def smooth_relu(preact):
    positive = jnp.maximum(preact, 0.0)
    return jnp.where(
        positive < KNEE_WIDTH, positive * positive / (2.0 * KNEE_WIDTH), positive - 0.5 * KNEE_WIDTH
    )


def relu_slope(preact):
    return jnp.clip(preact / KNEE_WIDTH, 0.0, 1.0)


def local(taps, token_ids, enc_weight, enc_bias, dec_weight, dec_bias):
    tap_rows = taps[0]
    tokens_dev = tap_rows.shape[0]
    loss_scale = 1.0 / math.sqrt(tokens_dev * lax.axis_size("token"))
    keep_mask = (token_ids != BEGIN_TOKEN).astype(jnp.float32)
    partial_pre = jnp.dot(
        tap_rows,
        lax.all_gather(enc_weight[0], "token", axis=0, tiled=True),
        preferred_element_type=jnp.float32,
    )
    preact = lax.psum(partial_pre, "layer") + enc_bias[None, :]
    features = smooth_relu(preact).astype(jnp.bfloat16)
    dec_full = lax.all_gather(dec_weight[0], "token", axis=0, tiled=True)
    rebuilt_part = lax.dot_general(
        features, dec_full, (((1,), (1,)), ((), ())), preferred_element_type=jnp.float32
    )
    rebuilt = lax.psum(rebuilt_part, "latent") + dec_bias[0][None, :]
    residue = (loss_scale * keep_mask[:, None] * (rebuilt - tap_rows.astype(jnp.float32))).astype(
        jnp.bfloat16
    )
    colnorm = jnp.sqrt(jnp.sum(jnp.square(dec_full.astype(jnp.float32)), axis=0) + 1e-06)
    back_part = jnp.dot(residue, dec_full, preferred_element_type=jnp.float32)
    feat_back, norm_total = lax.psum((back_part, colnorm), "layer")
    feat_grads = feat_back + loss_scale * SPARSITY * keep_mask[:, None] * norm_total[None, :]
    pre_grads = (feat_grads * relu_slope(preact)).astype(jnp.bfloat16)
    activity = jnp.sum(keep_mask[:, None] * features.astype(jnp.float32), axis=0)
    penalty_scale = loss_scale * SPARSITY * activity / colnorm
    product = lax.dot_general(
        residue, features, (((0,), (0,)), ((), ())), preferred_element_type=jnp.float32
    )
    dec_grad = lax.psum_scatter(
        (product + dec_full.astype(jnp.float32) * penalty_scale[None, :]).astype(jnp.bfloat16),
        "token",
        scatter_dimension=0,
        tiled=True,
    )
    enc_grad = lax.psum_scatter(
        lax.dot_general(
            tap_rows, pre_grads, (((0,), (0,)), ((), ())), preferred_element_type=jnp.float32
        ).astype(jnp.bfloat16),
        "token",
        scatter_dimension=0,
        tiled=True,
    )
    return (enc_grad[None], dec_grad[None])


def solution(mesh):
    placed = (
        P("layer", "token", None),
        P("token"),
        P("layer", "token", "latent"),
        P("latent"),
        P("layer", "token", "latent"),
        P("layer", None),
    )
    return jax.shard_map(
        local,
        mesh=mesh,
        in_specs=placed,
        out_specs=(P("layer", "token", "latent"), P("layer", "token", "latent")),
        check_vma=False,
    )
```

profile of v0, /device:TPU:6, one launch (start us, length us, event | category | flops | bytes accessed | tf_op | source)
XLA Modules:
  0.0 1122.9 jit_solution(13959128137853227899)
XLA Ops:
  7.2 0.7 all-gather.5.cloned.1.call-update
  8.0 76.5 %all-gather.5.cloned.1.call-done = bf16[1,3584,256]{2,1,0:T(8,128)(2,1)} async-done(((bf16[1,448,256]{2,1,0:T(8,128)(2,1)}), bf16[1,3584,256]{2,1,0:T(8,128)(2,1)}) %all-gather.5.cloned.1.call-update) | async-done | bytes 1835024 | tf_op jit(solution)/shard_map/all_gather | solution.py:30
  84.5 3.3 fusion.7
  87.8 0.7 all-gather.7.cloned.1.call-update
  88.5 34.3 %all-reduce.4.cloned.1.call-done = f32[224,256]{1,0:T(8,128)} async-done(((f32[224,256]{1,0:T(8,128)}), f32[224,256]{1,0:T(8,128)}) %all-reduce.4.cloned.1.call-update) | async-done | bytes 229392 | tf_op jit(solution)/shard_map/psum | solution.py:33
  122.9 1.6 multiply_reduce_fusion
  124.5 71.8 %all-gather.7.cloned.1.call-done = bf16[1,3584,256]{2,1,0:T(8,128)(2,1)} async-done(((bf16[1,448,256]{2,1,0:T(8,128)(2,1)}), bf16[1,3584,256]{2,1,0:T(8,128)(2,1)}) %all-gather.7.cloned.1.call-update) | async-done | bytes 1835024 | tf_op jit(solution)/shard_map/all_gather | solution.py:35
  196.3 3.9 fusion.5
  200.3 0.6 copy-done.4
  200.9 0.6 reduce
  202.1 692.7 %all-reduce.6.cloned.1.call-done = f32[224,3584]{1,0:T(8,128)} async-done(((f32[224,3584]{1,0:T(8,128)}), f32[224,3584]{1,0:T(8,128)}) %all-reduce.6.cloned.1.call-update) | async-done | bytes 3211280 | tf_op jit(solution)/shard_map/psum | solution.py:39
  894.9 2.6 multiply_convert_fusion
  897.5 1.2 copy-done.2
  898.6 1.3 fusion.3
  901.2 3.1 psum.31
  904.4 60.8 %all-reduce.8.cloned.1.call-done = f32[224,256]{1,0:T(8,128)} async-done(((f32[224,256]{1,0:T(8,128)}), f32[224,256]{1,0:T(8,128)}) %all-reduce.8.cloned.1.call-update) | async-done | bytes 229392 | tf_op jit(solution)/shard_map/psum | solution.py:45
  965.2 3.1 fusion.1
  968.2 3.8 copy.10
  972.1 1.3 copy-done.3
  973.5 2.6 fusion
  976.1 69.4 %reduce-scatter.7.cloned.1.call-done = bf16[448,256]{1,0:T(8,128)(2,1)} async-done(((bf16[3584,256]{1,0:T(8,128)(2,1)}), bf16[448,256]{1,0:T(8,128)(2,1)}) %reduce-scatter.7.cloned.1.call-update) | async-done | bytes 229392
  1045.5 1.1 copy.11
  1046.6 0.8 copy.9
  1047.4 68.7 %reduce-scatter.5.cloned.1.call-done = bf16[448,256]{1,0:T(8,128)(2,1)} async-done(((bf16[3584,256]{1,0:T(8,128)(2,1)}), bf16[448,256]{1,0:T(8,128)(2,1)}) %reduce-scatter.5.cloned.1.call-update) | async-done | bytes 229392 | tf_op jit(solution)/shard_map/reduce_scatter | solution.py:53
  (29 shorter events, 2.2 us)
Async XLA Ops:
  7.2 77.3 %all-gather.5.cloned.1.call-start = ((), (), s32[]{:S(2)}) async-start(), calls=%async_computation.6 | async-start | bytes 2064384 | tf_op jit(solution)/shard_map/all_gather | solution.py:30
  7.9 80.6 %copy-start.6 = (s32[224]{0:T(256)S(1)}, s32[224]{0:T(256)}, u32[]{:S(2)}) copy-start(s32[224]{0:T(256)} %param.7) | copy-start | bytes 2692
  7.9 115.0 %copy-start.7 = (f32[256]{0:T(256)S(1)}, f32[256]{0:T(256)}, u32[]{:S(2)}) copy-start(f32[256]{0:T(256)} %param.9) | copy-start | bytes 3076
  7.9 114.9 %all-reduce.4.cloned.1.call-start = ((), (), s32[]{:S(2)}) async-start(), calls=%async_computation.2 | async-start | bytes 458752 | tf_op jit(solution)/shard_map/psum | solution.py:33
  87.7 108.5 %all-gather.7.cloned.1.call-start = ((), (), s32[]{:S(2)}) async-start(), calls=%async_computation.7 | async-start | bytes 2064384 | tf_op jit(solution)/shard_map/all_gather | solution.py:35
  88.5 806.4 %all-reduce.6.cloned.1.call-start = ((), (), s32[]{:S(2)}) async-start(), calls=%async_computation.3 | async-start | bytes 6422528 | tf_op jit(solution)/shard_map/psum | solution.py:39
  200.2 0.7 copy-start.4
  200.2 694.7 %copy-start.1 = (bf16[1,224,3584]{2,1,0:T(8,128)(2,1)S(1)}, bf16[1,224,3584]{2,1,0:T(8,128)(2,1)}, u32[]{:S(2)}) copy-start(bf16[1,224,3584]{2,1,0:T(8,128)(2,1)} %param.6) | copy-start | bytes 4816900
  200.2 765.0 %all-reduce.8.cloned.1.call-start = ((), (), s32[]{:S(2)}) async-start(), calls=%async_computation.4 | async-start | bytes 458752 | tf_op jit(solution)/shard_map/psum | solution.py:45
  894.9 3.7 copy-start
  897.5 1.2 copy-start.2
  899.9 145.6 %reduce-scatter.7.cloned.1.call-start = ((), (), s32[]{:S(2)}) async-start(), calls=%async_computation.8 | async-start | bytes 2064384
  900.0 0.7 copy-start.5
  972.0 1.4 copy-start.3
  972.1 144.0 %reduce-scatter.5.cloned.1.call-start = ((), (), s32[]{:S(2)}) async-start(), calls=%async_computation.5 | async-start | bytes 2064384 | tf_op jit(solution)/shard_map/reduce_scatter | solution.py:53
Sparse Core Ops, SparseCore 0:
  10.1 74.3 all-gather.4
  87.9 34.9 all-reduce.3
  125.0 71.2 all-gather.6
  200.3 694.4 all-reduce.5
  900.0 65.0 all-reduce.7
  972.2 73.2 reduce-scatter.6
  1049.2 66.8 reduce-scatter.4
where the time goes:
time: 1120 us
  waiting for transfers between devices  1080 us (96%)
  between operations  14.2 us (1%)
  matrix products  14.1 us (1%)
    psum x1, waiting for transfers between devices, local(): rebuilt = lax.psum(rebuilt_part, 'latent') + dec_bias[0][None, :]  693 us
    all_gather x1, waiting for transfers between devices, local(): lax.all_gather(enc_weight[0], 'token', axis=0, tiled=True)  76.5 us
    all_gather x1, waiting for transfers between devices, local(): dec_full = lax.all_gather(dec_weight[0], 'token', axis=0, tiled=True)  71.8 us
    unnamed x8, waiting for transfers between devices  70.8 us
    reduce_scatter x1, waiting for transfers between devices, local(): lax.psum_scatter((product + dec_full.astype(jnp.float32) * penalty_scale[...  68.7 us
    psum x1, waiting for transfers between devices, local(): feat_back, norm_total = lax.psum((back_part, colnorm), 'layer')  60.8 us
    psum x1, waiting for transfers between devices, local(): preact = lax.psum(partial_pre, 'layer') + enc_bias[None, :]  34.3 us
  transfers between devices with their start and end apart: 7, of which 7 were waited for; matrix products, arithmetic and copies ran while one was open for 1% of the time, Pallas kernels for 0%

commit v1 on v0

--- a/solution.py
+++ b/solution.py
@@ -30,7 +30,7 @@
         lax.all_gather(enc_weight[0], "token", axis=0, tiled=True),
         preferred_element_type=jnp.float32,
     )
-    preact = lax.psum(partial_pre, "layer") + enc_bias[None, :]
+    preact = jnp.sum(lax.all_gather(partial_pre, "layer"), axis=0) + enc_bias[None, :]
     features = smooth_relu(preact).astype(jnp.bfloat16)
     dec_full = lax.all_gather(dec_weight[0], "token", axis=0, tiled=True)
     rebuilt_part = lax.dot_general(

time: 1120 us -> 1080 us (0.964)
  waiting for transfers between devices: 1080 us -> 1030 us
    psum x1 -> x0, waiting for transfers between devices: 34.3 us -> none  [local(): preact = lax.psum(partial_pre, 'layer') + enc_bias[None, :]]
    unnamed x8 -> x7, waiting for transfers between devices: 70.8 us -> 70.6 us
  transfers between devices with their start and end apart: 7 -> 6, of which waited for: 7 -> 6; matrix products, arithmetic and copies ran while one was open for 1% -> 1% of each run, Pallas kernels for 0% -> 0%
where the time goes in v1:
time: 1080 us
  waiting for transfers between devices  1030 us (95%)
  between operations  14.2 us (1%)
  matrix products  13.4 us (1%)
    psum x1, waiting for transfers between devices, local(): rebuilt = lax.psum(rebuilt_part, 'latent') + dec_bias[0][None, :]  691 us
    all_gather x1, waiting for transfers between devices, local(): lax.all_gather(enc_weight[0], 'token', axis=0, tiled=True)  75.1 us
    unnamed x7, waiting for transfers between devices  70.6 us
    reduce_scatter x1, waiting for transfers between devices, local(): lax.psum_scatter((product + dec_full.astype(jnp.float32) * penalty_scale[...  68.5 us
    all_gather x1, waiting for transfers between devices, local(): dec_full = lax.all_gather(dec_weight[0], 'token', axis=0, tiled=True)  62.3 us
    psum x1, waiting for transfers between devices, local(): feat_back, norm_total = lax.psum((back_part, colnorm), 'layer')  60.8 us
  transfers between devices with their start and end apart: 6, of which 6 were waited for; matrix products, arithmetic and copies ran while one was open for 1% of the time, Pallas kernels for 0%

profile of v1, /device:TPU:6, one launch (start us, length us, event | category | flops | bytes accessed | tf_op | source)
XLA Modules:
  0.0 1077.0 jit_solution(7692575096615787914)
XLA Ops:
  7.2 0.7 all-gather.6.cloned.1.call-update
  7.9 0.7 all-gather.8.cloned.1.call-update
  8.7 0.7 fusion.20
  9.4 75.1 %all-gather.6.cloned.1.call-done = bf16[1,3584,256]{2,1,0:T(8,128)(2,1)} async-done(((bf16[1,448,256]{2,1,0:T(8,128)(2,1)}), bf16[1,3584,256]{2,1,0:T(8,128)(2,1)}) %all-gather.6.cloned.1.call-update) | async-done | bytes 1835024 | tf_op jit(solution)/shard_map/all_gather | solution.py:30
  84.5 2.6 fusion.7
  87.0 2.1 all-gather.1
  89.2 0.7 multiply_reduce_fusion
  89.9 62.3 %all-gather.8.cloned.1.call-done = bf16[1,3584,256]{2,1,0:T(8,128)(2,1)} async-done(((bf16[1,448,256]{2,1,0:T(8,128)(2,1)}), bf16[1,3584,256]{2,1,0:T(8,128)(2,1)}) %all-gather.8.cloned.1.call-update) | async-done | bytes 1835024 | tf_op jit(solution)/shard_map/all_gather | solution.py:35
  152.2 3.9 fusion.5
  156.8 0.6 reduce
  158.1 691.3 %all-reduce.3.cloned.1.call-done = f32[224,3584]{1,0:T(8,128)} async-done(((f32[224,3584]{1,0:T(8,128)}), f32[224,3584]{1,0:T(8,128)}) %all-reduce.3.cloned.1.call-update) | async-done | bytes 3211280 | tf_op jit(solution)/shard_map/psum | solution.py:39
  849.4 2.6 multiply_convert_fusion
  852.0 1.1 copy-done.2
  853.1 1.3 fusion.3
  855.7 3.2 psum.23
  858.9 60.8 %all-reduce.5.cloned.1.call-done = f32[224,256]{1,0:T(8,128)} async-done(((f32[224,256]{1,0:T(8,128)}), f32[224,256]{1,0:T(8,128)}) %all-reduce.5.cloned.1.call-update) | async-done | bytes 229392 | tf_op jit(solution)/shard_map/psum | solution.py:45
  919.7 3.0 fusion.1
  922.7 3.8 copy.11
  926.6 1.3 copy-done.3
  928.0 2.6 fusion
  930.6 69.1 %reduce-scatter.7.cloned.1.call-done = bf16[448,256]{1,0:T(8,128)(2,1)} async-done(((bf16[3584,256]{1,0:T(8,128)(2,1)}), bf16[448,256]{1,0:T(8,128)(2,1)}) %reduce-scatter.7.cloned.1.call-update) | async-done | bytes 229392
  999.7 1.1 copy.12
  1000.8 0.8 copy.10
  1001.6 68.5 %reduce-scatter.5.cloned.1.call-done = bf16[448,256]{1,0:T(8,128)(2,1)} async-done(((bf16[3584,256]{1,0:T(8,128)(2,1)}), bf16[448,256]{1,0:T(8,128)(2,1)}) %reduce-scatter.5.cloned.1.call-update) | async-done | bytes 229392 | tf_op jit(solution)/shard_map/reduce_scatter | solution.py:53
  (30 shorter events, 2.8 us)
Async XLA Ops:
  7.2 77.3 %all-gather.6.cloned.1.call-start = ((), (), s32[]{:S(2)}) async-start(), calls=%async_computation.5 | async-start | bytes 2064384 | tf_op jit(solution)/shard_map/all_gather | solution.py:30
  7.9 144.3 %all-gather.8.cloned.1.call-start = ((), (), s32[]{:S(2)}) async-start(), calls=%async_computation.6 | async-start | bytes 2064384 | tf_op jit(solution)/shard_map/all_gather | solution.py:35
  8.6 840.8 %all-reduce.3.cloned.1.call-start = ((), (), s32[]{:S(2)}) async-start(), calls=%async_computation.2 | async-start | bytes 6422528 | tf_op jit(solution)/shard_map/psum | solution.py:39
  9.4 79.8 %copy-start.8 = (f32[256]{0:T(256)S(1)}, f32[256]{0:T(256)}, u32[]{:S(2)}) copy-start(f32[256]{0:T(256)} %param.9) | copy-start | bytes 3076
  89.2 63.0 %copy-start.4 = (f32[224,256]{1,0:T(8,128)}, f32[224,256]{1,0:T(8,128)S(1)}, u32[]{:S(2)}) copy-start(f32[224,256]{1,0:T(8,128)S(1)} %reduce_sum.27) | copy-start | bytes 688132
  156.1 0.7 copy-start.5
  156.1 1.4 copy-start.7
  156.1 693.3 %copy-start.1 = (bf16[1,224,3584]{2,1,0:T(8,128)(2,1)S(1)}, bf16[1,224,3584]{2,1,0:T(8,128)(2,1)}, u32[]{:S(2)}) copy-start(bf16[1,224,3584]{2,1,0:T(8,128)(2,1)} %param.6) | copy-start | bytes 4816900
  156.2 763.5 %all-reduce.5.cloned.1.call-start = ((), (), s32[]{:S(2)}) async-start(), calls=%async_computation.3 | async-start | bytes 458752 | tf_op jit(solution)/shard_map/psum | solution.py:45
  849.4 3.7 copy-start
  852.0 1.2 copy-start.2
  854.4 145.3 %reduce-scatter.7.cloned.1.call-start = ((), (), s32[]{:S(2)}) async-start(), calls=%async_computation.7 | async-start | bytes 2064384
  854.5 0.6 copy-start.6
  926.5 1.4 copy-start.3
  926.6 143.6 %reduce-scatter.5.cloned.1.call-start = ((), (), s32[]{:S(2)}) async-start(), calls=%async_computation.4 | async-start | bytes 2064384 | tf_op jit(solution)/shard_map/reduce_scatter | solution.py:53
Sparse Core Ops, SparseCore 0:
  10.1 74.3 all-gather.5
  86.5 65.6 all-gather.7
  156.3 693.0 all-reduce.2
  854.6 65.0 all-reduce.4
  926.7 72.9 reduce-scatter.6
  1003.2 66.8 reduce-scatter.4
